TPU v7x, 32 devices: a whole 2x2x4 slice. The times are simulated.
32 devices in a mesh: dp: 4 (over y, core), ctx: 4 (over z), tp: 2 (over x).
Axes of the slice: x: 2, y: 2, z: 4, core: 2. Of those that a mesh axis runs over, the one named last changes fastest.
Arguments:
- tokens: bfloat16 [4, 1024, 8192], P('dp', 'ctx', 'tp'), may hold values from -6 to 6
- queries: bfloat16 [4, 1024, 8192], P('dp', 'ctx', 'tp'), may hold values from -180 to 180
- k_weight: bfloat16 [8192, 512], P('dp', 'tp'), may hold values from -0.0625 to 0.0625
- v_weight: bfloat16 [8192, 512], P('dp', 'tp'), may hold values from -0.0625 to 0.0625
- doc_blocks: int32 [4, 8], P('dp', 'ctx'), may hold values from 0 to 3, never falling along the last dimension, each value on 1 to 4 neighbouring positions
Outputs:
- context: bfloat16 [4, 1024, 8192], P('dp', 'ctx', 'tp')
Inputs may be any that keep to these rules, and one draw needn't show every extreme that they name: `doc_blocks`: along each sequence the document numbers never fall; each document covers 1 to 4 whole blocks, one exactly 4.
All inputs are finite; a program needn't handle non-finite values.
Results may differ from a plain program's by a relative error of at most 0.012.
The roundings to bfloat16 on the way count: a program that leaves them out, or rounds other values in their place, can miss the bound.
Values may be sent and summed in bfloat16 or wider, within the bound.
A program may use at most 192 MiB of HBM per device.

v0:
```python
import math

import jax
import jax.numpy as jnp
from jax import lax
from jax.sharding import PartitionSpec as P

HD = 128
BLOCK = 128


ROPE_BASE = 500000.0
YARN_FACTOR = 16.0
PRETRAIN_CONTEXT = 8192.0
BETA_FAST = 32.0
BETA_SLOW = 1.0
ATTN_FACTOR = (1.0 + 0.1 * math.log(16.0)) ** 2
MASKED_SCORE = -1e30


def yarn_tables(positions):
    counter = jnp.arange(HD // 2, dtype=jnp.float32)
    base_freq = ROPE_BASE ** (-2.0 * counter / HD)
    wave_ratio = PRETRAIN_CONTEXT * base_freq / (2.0 * math.pi)
    ramp_value = jnp.clip((wave_ratio - BETA_SLOW) / (BETA_FAST - BETA_SLOW), 0.0, 1.0)
    frequency = ramp_value * base_freq + (1.0 - ramp_value) * base_freq / YARN_FACTOR
    angles = positions.astype(jnp.float32)[:, None] * frequency[None, :]
    cosine = jnp.cos(angles)
    sine_table = jnp.sin(angles)
    return (
        jnp.concatenate([cosine, cosine], axis=-1),
        jnp.concatenate([sine_table, sine_table], axis=-1),
    )


def rotate(vectors, cosine, sine_table):
    half_width = vectors.shape[-1] // 2
    lower_half = vectors[..., :half_width]
    upper_half = vectors[..., half_width:]
    turned = jnp.concatenate([-upper_half, lower_half], axis=-1)
    return vectors * cosine[:, None, :] + turned * sine_table[:, None, :]


def collect_features(local_tokens):
    return lax.all_gather(local_tokens, "tp", axis=1, tiled=True)


def body(tokens, queries, k_weight, v_weight, doc_blocks):
    local_tokens = tokens[0]
    row_count = local_tokens.shape[0]
    ctx_rank = lax.axis_index("ctx")
    all_docs = lax.all_gather(doc_blocks[0], "ctx", axis=0, tiled=True)
    kv_width = k_weight.shape[1]
    kv_heads = kv_width // HD
    whole = collect_features(local_tokens)
    pieces = (
        lax.all_gather(k_weight, "dp", axis=0, tiled=True),
        lax.all_gather(v_weight, "dp", axis=0, tiled=True),
    )
    height = pieces[0].shape[0]
    key_proj = jnp.dot(whole, pieces[0], preferred_element_type=jnp.float32)
    value_proj = jnp.dot(whole, pieces[1], preferred_element_type=jnp.float32)
    positions = ctx_rank * row_count + jnp.arange(row_count, dtype=jnp.int32)
    cosine, sine_table = yarn_tables(positions)
    key_rows = (
        rotate(key_proj.reshape(row_count, kv_heads, HD), cosine, sine_table)
        .reshape(row_count, kv_width)
        .astype(jnp.bfloat16)
    )
    value_rows = value_proj.astype(jnp.bfloat16)
    local_queries = queries[0]
    query_heads = local_queries.shape[1] // HD
    group_size = query_heads // kv_heads
    query_rot = (
        (
            rotate(
                local_queries.astype(jnp.float32).reshape(row_count, query_heads, HD),
                cosine,
                sine_table,
            )
            * (ATTN_FACTOR / math.sqrt(HD))
        )
        .reshape(row_count, query_heads * HD)
        .astype(jnp.bfloat16)
    )
    token_docs = jnp.repeat(all_docs, BLOCK)
    query_total = query_rot.shape[0]
    query_docs = token_docs[positions]
    grouped = query_rot.reshape(query_total, kv_heads, group_size, HD)
    start_max = jnp.full((kv_heads, group_size, query_total), MASKED_SCORE, jnp.float32)
    start_sum = jnp.zeros((kv_heads, group_size, query_total), jnp.float32)
    start_acc = jnp.zeros((kv_heads, group_size, query_total, HD), jnp.float32)
    key_piece = lax.all_gather(key_rows, "ctx", axis=0, tiled=True)
    value_piece = lax.all_gather(value_rows, "ctx", axis=0, tiled=True)
    height = key_piece.shape[0]
    key_pos = jnp.arange(height, dtype=jnp.int32)
    visible = (key_pos[None, :] <= positions[:, None]) & (
        token_docs[None, :] == query_docs[:, None]
    )

    def update(state):
        running_max, running_sum, running_acc = state
        scores = jnp.einsum(
            "qkgd,nkd->kgqn",
            grouped,
            key_piece.reshape(height, kv_heads, HD),
            preferred_element_type=jnp.float32,
        )
        scores = jnp.where(visible, scores, MASKED_SCORE)
        new_max = jnp.maximum(running_max, jnp.max(scores, axis=-1))
        weights = jnp.where(visible, jnp.exp(scores - new_max[..., None]), 0.0)
        new_sum = jnp.sum(weights, axis=-1)
        new_acc = jnp.einsum(
            "kgqn,nkd->kgqd",
            weights.astype(jnp.bfloat16),
            value_piece.reshape(height, kv_heads, HD),
            preferred_element_type=jnp.float32,
        )
        return (new_max, new_sum, new_acc)

    def unchanged(state):
        return state

    final_max, final_sum, final_acc = lax.cond(
        jnp.any(visible), update, unchanged, (start_max, start_sum, start_acc)
    )
    attended = final_acc / final_sum[..., None]
    context = (
        attended.transpose(2, 0, 1, 3).reshape(query_total, query_heads * HD).astype(jnp.bfloat16)
    )
    return context[None]


def solution(mesh):
    placed = (
        P("dp", "ctx", "tp"),
        P("dp", "ctx", "tp"),
        P("dp", "tp"),
        P("dp", "tp"),
        P("dp", "ctx"),
    )
    return jax.shard_map(
        body, mesh=mesh, in_specs=placed, out_specs=P("dp", "ctx", "tp"), check_vma=False
    )
```

profile of v0, /device:TPU:0, one launch (start us, length us, event | category | flops | bytes accessed | tf_op | source)
XLA Modules:
  0.0 219.2 jit_solution(14017968710612039538)
XLA Ops:
  6.5 0.7 all-gather.10.cloned.1.call-update
  7.3 0.7 all-gather.6.cloned.1.call-update
  10.1 9.9 %all-reduce = s32[8]{0:T(128)S(1)} all-reduce(s32[8]{0:T(128)S(1)} %bitcast_dynamic-update-slice_fusion), channel_id=2, replica_groups=mesh['dp'=4,'ctx'=4,'tp'=2] {'ctx'}, use_global_device_ids=true, to_apply=%add | all-reduce | flops 8 | bytes 64
  20.0 3.4 %copy.18 = bf16[1,256,4096]{1,2,0:T(8,128)(2,1)S(1)} copy(bf16[1,256,4096]{2,1,0:T(8,128)(2,1)} %param.8) | data formatting | bytes 4194304 | tf_op args[1]
  23.4 2.3 %convert_element_type.65 = f32[1,256,4096]{1,2,0:T(8,128)} convert(bf16[1,256,4096]{1,2,0:T(8,128)(2,1)S(1)} %copy.18) | non-fusion elementwise | flops 1048576 | bytes 6291456 | tf_op jit(solution)/shard_map/convert_element_type | solution.py:77
  25.8 1.4 gather_fusion
  27.2 0.9 fusion.17
  29.1 2.5 %slice_negate_fusion = (f32[256,32,64]{0,2,1:T(8,128)S(1)}, f32[256,32,64]{0,2,1:T(8,128)S(1)}) fusion(f32[256,32,128]{0,2,1:T(8,128)} %bitcast.50), kind=kLoop, calls=%fused_computation.19 | loop fusion | flops 524288 | bytes 8388608 | tf_op jit(solution)/shard_map/neg | solution.py:40
  32.1 1.7 copy-done
  33.8 1.1 multiply_convert_fusion
  34.9 33.5 %all-gather.10.cloned.1.call-done = bf16[1,256,8192]{2,1,0:T(8,128)(2,1)} async-done(((bf16[1,256,4096]{2,1,0:T(8,128)(2,1)}), bf16[1,256,8192]{2,1,0:T(8,128)(2,1)}) %all-gather.10.cloned.1.call-update) | async-done | bytes 4194320 | tf_op jit(solution)/shard_map/all_gather | solution.py:45
  68.4 36.1 %all-gather.6.cloned.1.call-done = bf16[8192,256]{1,0:T(8,128)(2,1)} async-done(((bf16[2048,256]{1,0:T(8,128)(2,1)}), bf16[8192,256]{1,0:T(8,128)(2,1)}) %all-gather.6.cloned.1.call-update) | async-done | bytes 4194320 | tf_op jit(solution)/shard_map/all_gather | solution.py:57
  104.5 5.2 %fusion.11 = f32[256,256]{0,1:T(8,128)S(1)} fusion(bf16[8192,256]{1,0:T(8,128)(2,1)} %all-gather.6.cloned.1.call-done, bf16[1,256,8192]{2,1,0:T(8,128)(2,1)} %all-gather.10.cloned.1.call-done), kind=kOutput, calls=%fused_computation.15 | convolution fusion | flops 1073741824 | bytes 8650752 | tf_op jit(solution)/shard_map/dot_general | solution.py:61
  109.8 16.1 %all_gather.21 = bf16[1024,256]{0,1:T(8,128)(2,1)S(1)} all-gather(bf16[256,256]{0,1:T(8,128)(2,1)S(1)} %fusion.18), channel_id=1, replica_groups=mesh['dp'=4,'ctx'=4,'tp'=2] {'ctx'}, dimensions={0}, use_global_device_ids=true | all-gather | bytes 655360 | tf_op jit(solution)/shard_map/all_gather | solution.py:93
  125.8 14.7 %all-gather.8.cloned.1.call-done = bf16[8192,256]{1,0:T(8,128)(2,1)} async-done(((bf16[2048,256]{1,0:T(8,128)(2,1)}), bf16[8192,256]{1,0:T(8,128)(2,1)}) %all-gather.8.cloned.1.call-update) | async-done | bytes 4194320 | tf_op jit(solution)/shard_map/all_gather | solution.py:58
  140.5 4.7 %fusion.14 = bf16[256,256]{1,0:T(8,128)(2,1)S(1)} fusion(bf16[8192,256]{1,0:T(8,128)(2,1)} %all-gather.8.cloned.1.call-done, bf16[1,256,8192]{2,1,0:T(8,128)(2,1)} %all-gather.10.cloned.1.call-done), kind=kOutput, calls=%fused_computation.21 | convolution fusion | flops 1073807360 | bytes 8519680 | tf_op jit(solution)/shard_map/dot_general | solution.py:62
  145.3 16.1 %all_gather.23 = bf16[1024,256]{1,0:T(8,128)(2,1)S(1)} all-gather(bf16[256,256]{1,0:T(8,128)(2,1)S(1)} %fusion.14), channel_id=1, replica_groups=mesh['dp'=4,'ctx'=4,'tp'=2] {'ctx'}, dimensions={0}, use_global_device_ids=true | all-gather | bytes 655360 | tf_op jit(solution)/shard_map/all_gather | solution.py:94
  161.3 44.8 %conditional.1 = (f32[2,16,256]{2,1,0:T(8,128)S(1)}, f32[2,16,256,128]{3,2,1,0:T(8,128)}) conditional(s32[]{:T(128)} %convert_element_type.53, () %tuple.13, (pred[256,1024]{0,1:T(8,128)(4,1)S(1)}, bf16[1024,256]{0,1:T(8,128)(2,1)S(1)}, bf16[256,2,16,128]{0,3,2,1:T(8,128)(2,1)S(1)}, bf16[1024,256]{1,0:T(8,128)(2,1)S(1)}) %tuple.14), branch_computations={%region_1.2_spmd, %region_2.5_spmd} | conditional | flops 4378845184 | bytes 110034960 | solution.py:124
  161.3 13.1 %fusion = (f32[2,16,256]{2,1,0:T(8,128)S(1)}, f32[2,1024,256,16]{2,1,3,0:T(8,128)}) fusion(pred[256,1024]{0,1:T(8,128)(4,1)S(1)} %get-tuple-element.13, bf16[1024,2,128,1]{0,2,3,1:T(8,128)(2,1)S(1)} %bitcast.54, bf16[256,2,16,128]{0,3,2,1:T(8,128)(2,1)S(1)} %get-tuple-element.27), kind=kOutput, calls=%fused_computation.3 | convolution fusion | flops 2164252672 | bytes 36470784 | tf_op jit(solution)/shard_map/cond/branch_1_fun/qkgd,nkd->kgqn/dot_general | solution.py:103
  174.6 17.1 %fusion.3 = f32[2,16,256,128]{3,2,1,0:T(8,128)} fusion(f32[2,1024,256,16]{2,1,3,0:T(8,128)} %get-tuple-element.30, f32[2,16,256]{2,1,0:T(8,128)S(1)} %broadcast_maximum_fusion, pred[256,1024]{0,1:T(8,128)(4,1)S(1)} %get-tuple-element.13, bf16[1024,2,128,1]{2,1,0,3:T(2,128)(2,1)S(1)} %bitcast.55), kind=kOutput, calls=%fused_computation.6 | convolution fusion | flops 2181038080 | bytes 38567936 | tf_op jit(solution)/shard_map/cond/branch_1_fun/kgqn,nkd->kgqd/dot_general | solution.py:113
  191.7 14.5 %fusion.2 = f32[2,16,256]{2,1,0:T(8,128)S(1)} fusion(f32[2,1024,256,16]{2,1,3,0:T(8,128)} %get-tuple-element.30, f32[2,16,256]{2,1,0:T(8,128)S(1)} %broadcast_maximum_fusion, pred[256,1024]{0,1:T(8,128)(4,1)S(1)} %get-tuple-element.13), kind=kLoop, calls=%fused_computation.5 | loop fusion | flops 33546240 | bytes 33882112 | tf_op jit(solution)/shard_map/cond/branch_1_fun/reduce_sum | solution.py:112
  206.1 2.9 %fusion.13 = bf16[256,2,16,128]{3,0,2,1:T(8,128)(2,1)S(1)} fusion(f32[2,16,256,128]{3,2,1,0:T(8,128)} %get-tuple-element.19, f32[2,16,256]{2,1,0:T(8,128)S(1)} %get-tuple-element.20), kind=kLoop, calls=%fused_computation.20 | loop fusion | flops 2097152 | bytes 6324224 | tf_op jit(solution)/shard_map/convert_element_type | solution.py:129
  209.0 1.4 copy.21
  210.4 2.3 %convert_element_type.64 = bf16[1,256,4096]{2,1,0:T(8,128)(2,1)} reshape(bf16[256,2,16,128]{3,2,1,0:T(8,128)(2,1)S(1)} %copy.21) | data formatting | bytes 4194304 | tf_op jit(solution)/shard_map/convert_element_type | solution.py:129
  (26 shorter events, 2.6 us)
Async XLA Ops:
  6.5 2.2 %copy-start.2 = (u32[32]{0:T(128)S(1)}, u32[32]{0:T(128)}, u32[]{:S(2)}) copy-start(u32[32]{0:T(128)} %constant.56) | copy-start | bytes 388
  6.5 3.5 %copy-start.1 = (s32[1,2]{1,0:T(1,128)S(1)}, s32[1,2]{1,0:T(1,128)}, u32[]{:S(2)}) copy-start(s32[1,2]{1,0:T(1,128)} %param.11) | copy-start | bytes 28
  6.5 61.8 %all-gather.10.cloned.1.call-start = ((), (), s32[]{:S(2)}) async-start(), calls=%async_computation.2 | async-start | bytes 6291456 | tf_op jit(solution)/shard_map/all_gather | solution.py:45
  7.3 97.2 %all-gather.6.cloned.1.call-start = ((), (), s32[]{:S(2)}) async-start(), calls=%async_computation | async-start | bytes 5242880 | tf_op jit(solution)/shard_map/all_gather | solution.py:57
  8.0 132.5 %all-gather.8.cloned.1.call-start = ((), (), s32[]{:S(2)}) async-start(), calls=%async_computation.1 | async-start | bytes 5242880 | tf_op jit(solution)/shard_map/all_gather | solution.py:58
  31.6 2.2 copy-start
Sparse Core Ops, SparseCore 0:
  8.9 59.4 all-gather.9
  69.9 34.4 all-gather.5
  106.0 34.4 all-gather.7
where the time goes:
time: 220 us; the launch traced here: 219 us
  waiting for transfers between devices  86.3 us (39%)
  blocking collectives  42 us (19%)
  matrix products  40.1 us (18%)
  other arithmetic  25 us (11%)
  between operations  14.6 us (7%)
  local copies, waits for them, and re-layouts  11 us (5%)
    all_gather x1, waiting for transfers between devices, body(): lax.all_gather(k_weight, 'dp', axis=0, tiled=True)  36.1 us
    all_gather x1, waiting for transfers between devices, collect_features(): return lax.all_gather(local_tokens, 'tp', axis=1, tiled=True)  33.5 us
    dot_general x1, matrix products, update(): jnp.einsum('kgqn,nkd->kgqd', weights.astype(jnp.bfloat16), value_piece.re...  17.1 us
    all_gather x1, blocking collectives, body(): value_piece = lax.all_gather(value_rows, 'ctx', axis=0, tiled=True)  16.1 us
    all_gather x1, blocking collectives, body(): key_piece = lax.all_gather(key_rows, 'ctx', axis=0, tiled=True)  16.1 us
    all_gather x1, waiting for transfers between devices, body(): lax.all_gather(v_weight, 'dp', axis=0, tiled=True)  14.7 us
    reduce_sum x1, other arithmetic, update(): new_sum = jnp.sum(weights, axis=-1)  14.5 us
    dot_general x1, matrix products, update(): jnp.einsum('qkgd,nkd->kgqn', grouped, key_piece.reshape(height, kv_heads,...  13.1 us
  transfers between devices with their start and end apart: 3, of which 3 were waited for; matrix products, arithmetic and copies ran while one was open for 8% of the time, Pallas kernels for 0%

commit v1 on v0

v1 whole, which is shorter than its diff:
```python
import functools
import math

import jax
import jax.numpy as jnp
import numpy as np
from jax import lax
from jax.experimental import pallas as pl
from jax.experimental.pallas import tpu as pltpu
from jax.sharding import PartitionSpec as P

HD = 128
BLOCK = 128
STEPS = 4
HEADS_AT_ONCE = 4

ROPE_BASE = 500000.0
YARN_FACTOR = 16.0
PRETRAIN_CONTEXT = 8192.0
BETA_FAST = 32.0
BETA_SLOW = 1.0
ATTN_FACTOR = (1.0 + 0.1 * math.log(16.0)) ** 2
MASKED_SCORE = -1e30
MESH = pl.DeviceIdType.MESH


def yarn_frequency():
    counter = np.arange(HD // 2, dtype=np.float64)
    base_freq = ROPE_BASE ** (-2.0 * counter / HD)
    wave_ratio = PRETRAIN_CONTEXT * base_freq / (2.0 * math.pi)
    ramp = np.clip((wave_ratio - BETA_SLOW) / (BETA_FAST - BETA_SLOW), 0.0, 1.0)
    frequency = ramp * base_freq + (1.0 - ramp) * base_freq / YARN_FACTOR
    return np.concatenate([frequency, frequency]).astype(np.float32)


def kernel(
    sizes,
    tok_hbm, q_hbm, kw_hbm, vw_hbm, freq_ref, docs_ref,
    out_ref,
    tok, qraw, qrot, wk, wv, acc, kv, docs, cos_ref, sin_ref,
    loc_sem, y_send, y_recv, s_send, s_recv, f_send, f_recv, t_send, t_recv,
    kv_send, kv_recv, d_send, d_recv,
):
    dp, n_ctx, tp = sizes
    groups = dp // 2
    pieces = dp // tp
    rows = q_hbm.shape[0]
    deep = kw_hbm.shape[0]
    part = deep // STEPS
    kvw = kw_hbm.shape[1]
    kv_heads = kvw // HD
    heads = q_hbm.shape[1] // HD
    back = docs.shape[0] - 1
    nb = rows // BLOCK
    span = nb * n_ctx // 2
    me_dp = lax.axis_index("dp")
    me_ctx = lax.axis_index("ctx")
    me_tp = lax.axis_index("tp")
    group = me_dp // 2
    core = me_dp % 2
    sib = group * 2 + (1 - core)

    def remote(src, dst, send, recv, where):
        return pltpu.make_async_remote_copy(
            src_ref=src, dst_ref=dst, send_sem=send, recv_sem=recv,
            device_id=where, device_id_type=MESH,
        )

    locals_ = [
        pltpu.make_async_copy(q_hbm, qraw, loc_sem.at[0]),
        pltpu.make_async_copy(kw_hbm, wk.at[me_dp], loc_sem.at[1]),
        pltpu.make_async_copy(vw_hbm, wv.at[me_dp], loc_sem.at[2]),
    ]
    for j in range(pieces):
        locals_.append(
            pltpu.make_async_copy(
                tok_hbm.at[:, pl.ds(j * deep, deep)],
                tok.at[me_tp * pieces + j],
                loc_sem.at[3 + j],
            )
        )
    for one in locals_:
        one.start()

    barrier = pltpu.get_barrier_semaphore()
    fixed = 0
    for r in range(1, groups):
        other = lax.rem(group + r, groups) * 2 + core
        pl.semaphore_signal(barrier, inc=1, device_id={"dp": other}, device_id_type=MESH)
        fixed += 1
    pl.semaphore_signal(barrier, inc=1, device_id={"dp": sib}, device_id_type=MESH)
    fixed += 1
    for r in range(1, tp):
        pl.semaphore_signal(
            barrier, inc=1, device_id={"tp": lax.rem(me_tp + r, tp)}, device_id_type=MESH
        )
        fixed += 1
    for d in range(1, back + 1):
        @pl.when(me_ctx + d < n_ctx)
        def _():
            pl.semaphore_signal(barrier, inc=1, device_id={"ctx": me_ctx + d}, device_id_type=MESH)

        @pl.when(me_ctx - d >= 0)
        def _():
            pl.semaphore_signal(barrier, inc=1, device_id={"ctx": me_ctx - d}, device_id_type=MESH)
    peers = fixed
    for d in range(1, back + 1):
        peers = peers + jnp.where(me_ctx + d < n_ctx, 1, 0) + jnp.where(me_ctx - d >= 0, 1, 0)
    pl.semaphore_wait(barrier, peers)

    started = []
    y_in, s_in, t_in = {}, {}, {}
    for i in range(STEPS):
        cut = pl.ds(i * part, part)
        for r in range(1, groups):
            to = lax.rem(group + r, groups) * 2 + core
            source = lax.rem(group + groups - r, groups) * 2 + core
            for w, (hbm, buf) in enumerate(((kw_hbm, wk), (vw_hbm, wv))):
                copy = remote(
                    hbm.at[cut], buf.at[me_dp, cut],
                    y_send.at[r - 1, i, w], y_recv.at[r - 1, i, w], {"dp": to},
                )
                copy.start()
                started.append(copy)
                y_in[r, i, w] = remote(
                    hbm.at[cut], buf.at[source, cut],
                    y_send.at[r - 1, i, w], y_recv.at[r - 1, i, w], {"dp": to},
                )
        for r in range(1, tp):
            to = lax.rem(me_tp + r, tp)
            source = lax.rem(me_tp + tp - r, tp)
            for j in range(pieces):
                copy = remote(
                    tok_hbm.at[:, pl.ds(j * deep + i * part, part)],
                    tok.at[me_tp * pieces + j, :, cut],
                    t_send.at[r - 1, i, j], t_recv.at[r - 1, i, j], {"tp": to},
                )
                copy.start()
                started.append(copy)
                t_in[r, i, j] = remote(
                    tok_hbm.at[:, pl.ds(j * deep + i * part, part)],
                    tok.at[source * pieces + j, :, cut],
                    t_send.at[r - 1, i, j], t_recv.at[r - 1, i, j], {"tp": to},
                )
        if i == 0:
            for w, (hbm, buf) in enumerate(((kw_hbm, wk), (vw_hbm, wv))):
                copy = remote(
                    hbm, buf.at[me_dp], s_send.at[w], s_recv.at[w], {"dp": sib}
                )
                copy.start()
                started.append(copy)
                s_in[w] = remote(
                    hbm, buf.at[sib], s_send.at[w], s_recv.at[w], {"dp": sib}
                )

    def doc_copy(d):
        return remote(
            docs_ref, docs.at[back - d], d_send.at[d - 1], d_recv.at[d - 1], {"ctx": me_ctx + d}
        )

    def doc_in(d):
        return remote(
            docs_ref, docs.at[back - d], d_send.at[d - 1], d_recv.at[d - 1], {"ctx": me_ctx - d}
        )

    for d in range(1, back + 1):
        @pl.when(me_ctx + d < n_ctx)
        def _():
            doc_copy(d).start()

        @pl.when(me_ctx - d < 0)
        def _():
            docs[back - d] = jnp.full(docs.shape[1:], -1, jnp.int32)
            kv[back - d] = jnp.zeros(kv.shape[1:], kv.dtype)
    docs[back] = docs_ref[...]

    position = me_ctx * rows + lax.broadcasted_iota(jnp.int32, (rows, HD), 0)
    angle = position.astype(jnp.float32) * freq_ref[...]
    upper = lax.broadcasted_iota(jnp.int32, (rows, HD), 1) >= HD // 2
    cos_ref[...] = jnp.cos(angle)
    sine = jnp.sin(angle)
    sin_ref[...] = jnp.where(upper, sine, -sine)
    for one in locals_:
        one.wait()
    scale = ATTN_FACTOR / math.sqrt(HD)

    @pl.loop(0, heads)
    def _(h):
        u = qraw[:, pl.ds(pl.multiple_of(h * HD, HD), HD)].astype(jnp.float32)
        turned = u * cos_ref[...] + pltpu.roll(u, HD // 2, 1) * sin_ref[...]
        qrot[h] = (turned * scale).astype(jnp.bfloat16)

    acc[...] = jnp.zeros_like(acc)
    for w in range(2):
        s_in[w].wait_recv()

    for i in range(STEPS):
        cut = pl.ds(i * part, part)
        forwarded = []
        for r in range(1, groups):
            source = lax.rem(group + groups - r, groups) * 2 + core
            sib_source = lax.rem(group + groups - r, groups) * 2 + (1 - core)
            for w, buf in enumerate((wk, wv)):
                y_in[r, i, w].wait_recv()
                copy = remote(
                    buf.at[source, cut], buf.at[source, cut],
                    f_send.at[r - 1, i, w], f_recv.at[r - 1, i, w], {"dp": sib},
                )
                copy.start()
                started.append(copy)
                forwarded.append(
                    remote(
                        buf.at[sib_source, cut], buf.at[sib_source, cut],
                        f_send.at[r - 1, i, w], f_recv.at[r - 1, i, w], {"dp": sib},
                    )
                )
        for r in range(1, tp):
            for j in range(pieces):
                t_in[r, i, j].wait_recv()
        for copy in forwarded:
            copy.wait_recv()

        @pl.loop(0, dp)
        def _(p):
            x = tok[p, :, cut]
            acc[:, :kvw] += jnp.dot(x, wk[p, cut, :], preferred_element_type=jnp.float32)
            acc[:, kvw:] += jnp.dot(x, wv[p, cut, :], preferred_element_type=jnp.float32)

    for g in range(kv_heads):
        u = acc[:, g * HD:(g + 1) * HD]
        turned = u * cos_ref[...] + pltpu.roll(u, HD // 2, 1) * sin_ref[...]
        kv[back, g, :, :HD] = turned.astype(jnp.bfloat16)
        kv[back, g, :, HD:] = acc[:, kvw + g * HD:kvw + (g + 1) * HD].astype(jnp.bfloat16)

        for d in range(1, back + 1):
            @pl.when(me_ctx + d < n_ctx)
            def _():
                kv_copy(kv, kv_send, kv_recv, remote, back, span, nb, rows, g, d, me_ctx + d).start()

    for d in range(1, back + 1):
        @pl.when(me_ctx - d >= 0)
        def _():
            doc_in(d).wait_recv()

    wide = span * BLOCK
    keep = []
    for b in range(nb):
        first = back * nb + b + 1 - span
        mine = docs[back, 0:1, b * BLOCK:(b + 1) * BLOCK]
        key_docs = jnp.concatenate(
            [
                docs[(first + k) // nb, 0:1, ((first + k) % nb) * BLOCK:((first + k) % nb + 1) * BLOCK] - mine
                for k in range(span)
            ],
            axis=1,
        )
        column = lax.broadcasted_iota(jnp.int32, (BLOCK, wide), 1) - (span - 1) * BLOCK
        row = lax.broadcasted_iota(jnp.int32, (BLOCK, wide), 0)
        keep.append((column <= row) & (key_docs == 0))

    group_heads = heads // kv_heads
    for g in range(kv_heads):
        for d in range(1, back + 1):
            @pl.when(me_ctx - d >= 0)
            def _():
                kv_copy(kv, kv_send, kv_recv, remote, back, span, nb, rows, g, d, me_ctx - d).wait_recv()
        for b in range(nb):
            first = back * nb + b + 1 - span
            window = jnp.concatenate(
                [
                    kv[(first + k) // nb, g, ((first + k) % nb) * BLOCK:((first + k) % nb + 1) * BLOCK, :]
                    for k in range(span)
                ],
                axis=0,
            )
            keys, values = window[:, :HD], window[:, HD:]
            mask = keep[b]

            @pl.loop(0, group_heads // HEADS_AT_ONCE)
            def _(t):
                h0 = g * group_heads + t * HEADS_AT_ONCE
                q = qrot[pl.ds(h0, HEADS_AT_ONCE), b * BLOCK:(b + 1) * BLOCK, :]
                s = lax.dot_general(
                    q.reshape(HEADS_AT_ONCE * BLOCK, HD), keys,
                    (((1,), (1,)), ((), ())), preferred_element_type=jnp.float32,
                ).reshape(HEADS_AT_ONCE, BLOCK, wide)
                s = jnp.where(mask[None], s, MASKED_SCORE)
                top = jnp.max(s, axis=-1, keepdims=True)
                e = jnp.exp(s - top)
                total = jnp.sum(e, axis=-1, keepdims=True)
                mixed = jnp.dot(
                    e.astype(jnp.bfloat16).reshape(HEADS_AT_ONCE * BLOCK, wide), values,
                    preferred_element_type=jnp.float32,
                ).reshape(HEADS_AT_ONCE, BLOCK, HD)
                mixed = (mixed / total).astype(jnp.bfloat16)
                for k in range(HEADS_AT_ONCE):
                    out_ref[b * BLOCK:(b + 1) * BLOCK, pl.ds(pl.multiple_of((h0 + k) * HD, HD), HD)] = mixed[k]

    for copy in started:
        copy.wait_send()
    for d in range(1, back + 1):
        @pl.when(me_ctx + d < n_ctx)
        def _():
            doc_copy(d).wait_send()
            for g in range(kv_heads):
                kv_copy(kv, kv_send, kv_recv, remote, back, span, nb, rows, g, d, me_ctx + d).wait_send()


def kv_copy(kv, send, recv, remote, back, span, nb, rows, g, d, other):
    skip = max(0, d * nb + 1 - span) * BLOCK
    cut = pl.ds(skip, rows - skip)
    return remote(
        kv.at[back, g, cut], kv.at[back - d, g, cut],
        send.at[d - 1, g], recv.at[d - 1, g], {"ctx": other},
    )


def solution(mesh):
    dp, n_ctx, tp = mesh.shape["dp"], mesh.shape["ctx"], mesh.shape["tp"]

    def body(tokens, queries, k_weight, v_weight, doc_blocks):
        rows, width = tokens.shape[1], tokens.shape[2]
        deep, kvw = k_weight.shape
        heads = queries.shape[2] // HD
        nb = rows // BLOCK
        span = nb * n_ctx // 2
        back = -(-(span - 1) // nb)
        groups, pieces = dp // 2, dp // tp
        docs = jnp.broadcast_to(jnp.repeat(doc_blocks[0], BLOCK)[None, :], (8, rows))
        frequency = jnp.asarray(yarn_frequency()).reshape(1, HD)
        dma = pltpu.SemaphoreType.DMA
        anywhere = pl.BlockSpec(memory_space=pl.ANY)
        vmem = pl.BlockSpec(memory_space=pltpu.VMEM)
        out = pl.pallas_call(
            functools.partial(kernel, (dp, n_ctx, tp)),
            out_shape=jax.ShapeDtypeStruct((rows, heads * HD), jnp.bfloat16),
            in_specs=[anywhere] * 4 + [vmem] * 2,
            out_specs=vmem,
            scratch_shapes=[
                pltpu.VMEM((dp, rows, deep), jnp.bfloat16),
                pltpu.VMEM((rows, heads * HD), jnp.bfloat16),
                pltpu.VMEM((heads, rows, HD), jnp.bfloat16),
                pltpu.VMEM((dp, deep, kvw), jnp.bfloat16),
                pltpu.VMEM((dp, deep, kvw), jnp.bfloat16),
                pltpu.VMEM((rows, 2 * kvw), jnp.float32),
                pltpu.VMEM((back + 1, kvw // HD, rows, 2 * HD), jnp.bfloat16),
                pltpu.VMEM((back + 1, 8, rows), jnp.int32),
                pltpu.VMEM((rows, HD), jnp.float32),
                pltpu.VMEM((rows, HD), jnp.float32),
                dma((3 + pieces,)),
                dma((groups - 1, STEPS, 2)), dma((groups - 1, STEPS, 2)),
                dma((2,)), dma((2,)),
                dma((groups - 1, STEPS, 2)), dma((groups - 1, STEPS, 2)),
                dma((tp - 1, STEPS, pieces)), dma((tp - 1, STEPS, pieces)),
                dma((back, kvw // HD)), dma((back, kvw // HD)),
                dma((back,)), dma((back,)),
            ],
            compiler_params=pltpu.CompilerParams(
                collective_id=0, has_side_effects=True, vmem_limit_bytes=48 << 20
            ),
        )(tokens[0], queries[0], k_weight, v_weight, frequency, docs)
        return out[None]

    placed = (
        P("dp", "ctx", "tp"),
        P("dp", "ctx", "tp"),
        P("dp", "tp"),
        P("dp", "tp"),
        P("dp", "ctx"),
    )
    return jax.shard_map(
        body, mesh=mesh, in_specs=placed, out_specs=P("dp", "ctx", "tp"), check_vma=False
    )
```

time: 220 us -> 77.9 us (0.35)
  the two profiles are of different devices: /device:TPU:0 before, /device:TPU:27 now
where the time goes in v1:
time: 77.9 us; the launch traced here: 78 us
  Pallas kernels  72.9 us (94%)
  local copies, waits for them, and re-layouts  5.15 us (7%)
    pallas_call x1, Pallas kernels, body(): pl.pallas_call(functools.partial(kernel, (dp, n_ctx, tp)), out_shape=jax....  72.9 us
    unnamed x9, local copies, waits for them, and re-layouts  5.08 us

profile of v1, /device:TPU:27, one launch (start us, length us, event | category | flops | bytes accessed | tf_op | source)
XLA Modules:
  0.0 78.0 jit_solution(18441986177708104618)
XLA Ops:
  0.0 0.0 copy-start
  0.0 0.7 copy-done
  0.7 0.1 broadcast_bitcast_fusion
  0.7 0.0 copy-start.1
  0.7 1.2 %copy-done.1 = bf16[2048,256]{1,0:T(8,128)(2,1)S(1)} copy-done((bf16[2048,256]{1,0:T(8,128)(2,1)S(1)}, bf16[2048,256]{1,0:T(8,128)(2,1)}, u32[]{:S(2)}) %copy-start.1) | copy-done | bytes 1048600
  2.0 0.0 copy-start.2
  2.0 1.2 %copy-done.2 = bf16[2048,256]{1,0:T(8,128)(2,1)S(1)} copy-done((bf16[2048,256]{1,0:T(8,128)(2,1)S(1)}, bf16[2048,256]{1,0:T(8,128)(2,1)}, u32[]{:S(2)}) %copy-start.2) | copy-done | bytes 1048600
  3.2 0.0 copy-start.3
  3.2 0.7 copy-done.3
  3.8 72.9 %shard_map.64 = bf16[256,4096]{1,0:T(8,128)(2,1)S(1)} custom-call(bf16[256,4096]{1,0:T(8,128)(2,1)} %bitcast.8, bf16[256,4096]{1,0:T(8,128)(2,1)} %bitcast.9, bf16[2048,256]{1,0:T(8,128)(2,1)S(1)} %copy-done.1, bf16[2048,256]{1,0:T(8,128)(2,1)S(1)} %copy-done.2, f32[1,128]{1,0:T(1,128)S(1)} %copy-done.3, s32[8,256]{1,0:T(8,128)S(1)} %broadcast_in_dim.15.docs_ref), custom_call_target="tpu_custom_call" | custom-call | tf_op jit(solution)/shard_map/pallas_call | solution.py:334
  76.7 1.3 %copy.8 = bf16[1,256,4096]{2,1,0:T(8,128)(2,1)} copy(bf16[1,256,4096]{2,1,0:T(8,128)(2,1)S(1)} %bitcast.7) | data formatting | bytes 4194304
  (1 shorter events, 0.0 us)
Async XLA Ops:
  0.0 0.7 copy-start
  0.7 1.2 %copy-start.1 = (bf16[2048,256]{1,0:T(8,128)(2,1)S(1)}, bf16[2048,256]{1,0:T(8,128)(2,1)}, u32[]{:S(2)}) copy-start(bf16[2048,256]{1,0:T(8,128)(2,1)} %kw_hbm.1) | copy-start | bytes 3145732
  2.0 1.2 %copy-start.2 = (bf16[2048,256]{1,0:T(8,128)(2,1)S(1)}, bf16[2048,256]{1,0:T(8,128)(2,1)}, u32[]{:S(2)}) copy-start(bf16[2048,256]{1,0:T(8,128)(2,1)} %vw_hbm.1) | copy-start | bytes 3145732
  3.2 0.7 copy-start.3

commit v2 on v1

--- a/solution.py
+++ b/solution.py
@@ -3,7 +3,6 @@
 
 import jax
 import jax.numpy as jnp
-import numpy as np
 from jax import lax
 from jax.experimental import pallas as pl
 from jax.experimental.pallas import tpu as pltpu
@@ -12,7 +11,7 @@
 HD = 128
 BLOCK = 128
 STEPS = 4
-HEADS_AT_ONCE = 4
+HEADS_AT_ONCE = 8
 
 ROPE_BASE = 500000.0
 YARN_FACTOR = 16.0
@@ -24,20 +23,19 @@
 MESH = pl.DeviceIdType.MESH
 
 
-def yarn_frequency():
-    counter = np.arange(HD // 2, dtype=np.float64)
-    base_freq = ROPE_BASE ** (-2.0 * counter / HD)
-    wave_ratio = PRETRAIN_CONTEXT * base_freq / (2.0 * math.pi)
-    ramp = np.clip((wave_ratio - BETA_SLOW) / (BETA_FAST - BETA_SLOW), 0.0, 1.0)
-    frequency = ramp * base_freq + (1.0 - ramp) * base_freq / YARN_FACTOR
-    return np.concatenate([frequency, frequency]).astype(np.float32)
+def yarn_frequency(shape):
+    counter = lax.broadcasted_iota(jnp.int32, shape, 1) % (HD // 2)
+    base_freq = jnp.exp(counter.astype(jnp.float32) * (-2.0 * math.log(ROPE_BASE) / HD))
+    wave_ratio = base_freq * (PRETRAIN_CONTEXT / (2.0 * math.pi))
+    ramp = jnp.clip((wave_ratio - BETA_SLOW) / (BETA_FAST - BETA_SLOW), 0.0, 1.0)
+    return ramp * base_freq + (1.0 - ramp) * base_freq / YARN_FACTOR
 
 
 def kernel(
     sizes,
-    tok_hbm, q_hbm, kw_hbm, vw_hbm, freq_ref, docs_ref,
+    tok_hbm, q_hbm, kw_hbm, vw_hbm, docs_hbm,
     out_ref,
-    tok, qraw, qrot, wk, wv, acc, kv, docs, cos_ref, sin_ref,
+    tok, qraw, qrot, wk, wv, acc, kv, docs, docs_own, cos_ref, sin_ref,
     loc_sem, y_send, y_recv, s_send, s_recv, f_send, f_recv, t_send, t_recv,
     kv_send, kv_recv, d_send, d_recv,
 ):
@@ -79,6 +77,8 @@
                 loc_sem.at[3 + j],
             )
         )
+    docs_in = pltpu.make_async_copy(docs_hbm, docs_own, loc_sem.at[3 + pieces])
+    docs_in.start()
     for one in locals_:
         one.start()
 
@@ -110,7 +110,7 @@
 
     started = []
     y_in, s_in, t_in = {}, {}, {}
-    for i in range(STEPS):
+    def start_step(i):
         cut = pl.ds(i * part, part)
         for r in range(1, groups):
             to = lax.rem(group + r, groups) * 2 + core
@@ -142,27 +142,35 @@
                     tok.at[source * pieces + j, :, cut],
                     t_send.at[r - 1, i, j], t_recv.at[r - 1, i, j], {"tp": to},
                 )
-        if i == 0:
-            for w, (hbm, buf) in enumerate(((kw_hbm, wk), (vw_hbm, wv))):
-                copy = remote(
-                    hbm, buf.at[me_dp], s_send.at[w], s_recv.at[w], {"dp": sib}
-                )
-                copy.start()
-                started.append(copy)
-                s_in[w] = remote(
-                    hbm, buf.at[sib], s_send.at[w], s_recv.at[w], {"dp": sib}
-                )
+
+    start_step(0)
+    for w, (hbm, buf) in enumerate(((kw_hbm, wk), (vw_hbm, wv))):
+        copy = remote(
+            hbm, buf.at[me_dp], s_send.at[w], s_recv.at[w], {"dp": sib}
+        )
+        copy.start()
+        started.append(copy)
+        s_in[w] = remote(
+            hbm, buf.at[sib], s_send.at[w], s_recv.at[w], {"dp": sib}
+        )
+    start_step(1)
 
     def doc_copy(d):
         return remote(
-            docs_ref, docs.at[back - d], d_send.at[d - 1], d_recv.at[d - 1], {"ctx": me_ctx + d}
+            docs.at[back], docs.at[back - d], d_send.at[d - 1], d_recv.at[d - 1], {"ctx": me_ctx + d}
         )
 
     def doc_in(d):
         return remote(
-            docs_ref, docs.at[back - d], d_send.at[d - 1], d_recv.at[d - 1], {"ctx": me_ctx - d}
-        )
-
+            docs.at[back], docs.at[back - d], d_send.at[d - 1], d_recv.at[d - 1], {"ctx": me_ctx - d}
+        )
+
+    docs_in.wait()
+    lane = lax.broadcasted_iota(jnp.int32, docs.shape[1:], 1)
+    spread = jnp.broadcast_to(docs_own[0:1, 0:1], docs.shape[1:])
+    for b in range(1, nb):
+        spread = jnp.where(lane >= b * BLOCK, docs_own[0:1, b:b + 1], spread)
+    docs[back] = spread
     for d in range(1, back + 1):
         @pl.when(me_ctx + d < n_ctx)
         def _():
@@ -172,10 +180,9 @@
         def _():
             docs[back - d] = jnp.full(docs.shape[1:], -1, jnp.int32)
             kv[back - d] = jnp.zeros(kv.shape[1:], kv.dtype)
-    docs[back] = docs_ref[...]
 
     position = me_ctx * rows + lax.broadcasted_iota(jnp.int32, (rows, HD), 0)
-    angle = position.astype(jnp.float32) * freq_ref[...]
+    angle = position.astype(jnp.float32) * yarn_frequency((1, HD))
     upper = lax.broadcasted_iota(jnp.int32, (rows, HD), 1) >= HD // 2
     cos_ref[...] = jnp.cos(angle)
     sine = jnp.sin(angle)
@@ -220,6 +227,9 @@
         for copy in forwarded:
             copy.wait_recv()
 
+        if i + 2 < STEPS:
+            start_step(i + 2)
+
         @pl.loop(0, dp)
         def _(p):
             x = tok[p, :, cut]
@@ -231,8 +241,13 @@
         turned = u * cos_ref[...] + pltpu.roll(u, HD // 2, 1) * sin_ref[...]
         kv[back, g, :, :HD] = turned.astype(jnp.bfloat16)
         kv[back, g, :, HD:] = acc[:, kvw + g * HD:kvw + (g + 1) * HD].astype(jnp.bfloat16)
-
-        for d in range(1, back + 1):
+    for d in range(1, back + 1):
+        for g in range(kv_heads):
+            if d > 1:
+                @pl.when(me_ctx + d - 1 < n_ctx)
+                def _():
+                    kv_copy(kv, kv_send, kv_recv, remote, back, span, nb, rows, g, d - 1, me_ctx + d - 1).wait_send()
+        for g in range(kv_heads):
             @pl.when(me_ctx + d < n_ctx)
             def _():
                 kv_copy(kv, kv_send, kv_recv, remote, back, span, nb, rows, g, d, me_ctx + d).start()
@@ -259,13 +274,15 @@
         keep.append((column <= row) & (key_docs == 0))
 
     group_heads = heads // kv_heads
-    for g in range(kv_heads):
-        for d in range(1, back + 1):
-            @pl.when(me_ctx - d >= 0)
-            def _():
-                kv_copy(kv, kv_send, kv_recv, remote, back, span, nb, rows, g, d, me_ctx - d).wait_recv()
-        for b in range(nb):
-            first = back * nb + b + 1 - span
+    reached = [0] * kv_heads
+    for b in reversed(range(nb)):
+        first = back * nb + b + 1 - span
+        for g in range(kv_heads):
+            for d in range(reached[g] + 1, back - first // nb + 1):
+                @pl.when(me_ctx - d >= 0)
+                def _():
+                    kv_copy(kv, kv_send, kv_recv, remote, back, span, nb, rows, g, d, me_ctx - d).wait_recv()
+            reached[g] = max(reached[g], back - first // nb)
             window = jnp.concatenate(
                 [
                     kv[(first + k) // nb, g, ((first + k) % nb) * BLOCK:((first + k) % nb + 1) * BLOCK, :]
@@ -292,7 +309,7 @@
                     e.astype(jnp.bfloat16).reshape(HEADS_AT_ONCE * BLOCK, wide), values,
                     preferred_element_type=jnp.float32,
                 ).reshape(HEADS_AT_ONCE, BLOCK, HD)
-                mixed = (mixed / total).astype(jnp.bfloat16)
+                mixed = (mixed * (1.0 / total)).astype(jnp.bfloat16)
                 for k in range(HEADS_AT_ONCE):
                     out_ref[b * BLOCK:(b + 1) * BLOCK, pl.ds(pl.multiple_of((h0 + k) * HD, HD), HD)] = mixed[k]
 
@@ -302,8 +319,9 @@
         @pl.when(me_ctx + d < n_ctx)
         def _():
             doc_copy(d).wait_send()
-            for g in range(kv_heads):
-                kv_copy(kv, kv_send, kv_recv, remote, back, span, nb, rows, g, d, me_ctx + d).wait_send()
+            if d == back:
+                for g in range(kv_heads):
+                    kv_copy(kv, kv_send, kv_recv, remote, back, span, nb, rows, g, d, me_ctx + d).wait_send()
 
 
 def kv_copy(kv, send, recv, remote, back, span, nb, rows, g, d, other):
@@ -326,15 +344,13 @@
         span = nb * n_ctx // 2
         back = -(-(span - 1) // nb)
         groups, pieces = dp // 2, dp // tp
-        docs = jnp.broadcast_to(jnp.repeat(doc_blocks[0], BLOCK)[None, :], (8, rows))
-        frequency = jnp.asarray(yarn_frequency()).reshape(1, HD)
         dma = pltpu.SemaphoreType.DMA
-        anywhere = pl.BlockSpec(memory_space=pl.ANY)
+        hbm = pl.BlockSpec(memory_space=pltpu.HBM)
         vmem = pl.BlockSpec(memory_space=pltpu.VMEM)
         out = pl.pallas_call(
             functools.partial(kernel, (dp, n_ctx, tp)),
             out_shape=jax.ShapeDtypeStruct((rows, heads * HD), jnp.bfloat16),
-            in_specs=[anywhere] * 4 + [vmem] * 2,
+            in_specs=[hbm] * 5,
             out_specs=vmem,
             scratch_shapes=[
                 pltpu.VMEM((dp, rows, deep), jnp.bfloat16),
@@ -345,9 +361,10 @@
                 pltpu.VMEM((rows, 2 * kvw), jnp.float32),
                 pltpu.VMEM((back + 1, kvw // HD, rows, 2 * HD), jnp.bfloat16),
                 pltpu.VMEM((back + 1, 8, rows), jnp.int32),
+                pltpu.VMEM((1, nb), jnp.int32),
                 pltpu.VMEM((rows, HD), jnp.float32),
                 pltpu.VMEM((rows, HD), jnp.float32),
-                dma((3 + pieces,)),
+                dma((4 + pieces,)),
                 dma((groups - 1, STEPS, 2)), dma((groups - 1, STEPS, 2)),
                 dma((2,)), dma((2,)),
                 dma((groups - 1, STEPS, 2)), dma((groups - 1, STEPS, 2)),
@@ -356,9 +373,9 @@
                 dma((back,)), dma((back,)),
             ],
             compiler_params=pltpu.CompilerParams(
-                collective_id=0, has_side_effects=True, vmem_limit_bytes=48 << 20
+                collective_id=0, has_side_effects=True, vmem_limit_bytes=60 << 20
             ),
-        )(tokens[0], queries[0], k_weight, v_weight, frequency, docs)
+        )(tokens[0], queries[0], k_weight, v_weight, doc_blocks)
         return out[None]
 
     placed = (

time: 77.9 us -> 74.2 us (0.953)
  the two profiles are of different devices: /device:TPU:27 before, /device:TPU:0 now
where the time goes in v2:
time: 74.2 us; the launch traced here: 73.6 us
  Pallas kernels  70.4 us (95%)
  local copies, waits for them, and re-layouts  3.13 us (4%)
    pallas_call x1, Pallas kernels, body(): pl.pallas_call(functools.partial(kernel, (dp, n_ctx, tp)), out_shape=jax....  70.4 us
    unnamed x1, local copies, waits for them, and re-layouts  3.13 us

profile of v2, /device:TPU:0, one launch (start us, length us, event | category | flops | bytes accessed | tf_op | source)
XLA Modules:
  0.0 73.6 jit_solution(4110232926420291339)
XLA Ops:
  0.0 70.4 %shard_map.55 = bf16[256,4096]{1,0:T(8,128)(2,1)} custom-call(bf16[256,4096]{1,0:T(8,128)(2,1)} %bitcast.4, bf16[256,4096]{1,0:T(8,128)(2,1)} %bitcast.5, bf16[2048,256]{1,0:T(8,128)(2,1)} %kw_hbm.1, bf16[2048,256]{1,0:T(8,128)(2,1)} %vw_hbm.1, s32[1,2]{1,0:T(1,128)} %docs_hbm.1), custom_call_target="tpu_custom_call" | custom-call | tf_op jit(solution)/shard_map/pallas_call | solution.py:350
  70.5 3.1 %copy.7 = bf16[1,256,4096]{2,1,0:T(8,128)(2,1)} copy(bf16[1,256,4096]{2,1,0:T(8,128)(2,1)} %bitcast.3) | data formatting | bytes 4194304

commit v3 on v2

--- a/solution.py
+++ b/solution.py
@@ -36,7 +36,7 @@
     tok_hbm, q_hbm, kw_hbm, vw_hbm, docs_hbm,
     out_ref,
     tok, qraw, qrot, wk, wv, acc, kv, docs, docs_own, cos_ref, sin_ref,
-    loc_sem, y_send, y_recv, s_send, s_recv, f_send, f_recv, t_send, t_recv,
+    loc_sem, y_send, y_recv, s_send, s_recv, f_send, f_recv, z_send, z_recv, t_send, t_recv,
     kv_send, kv_recv, d_send, d_recv,
 ):
     dp, n_ctx, tp = sizes
@@ -109,51 +109,69 @@
     pl.semaphore_wait(barrier, peers)
 
     started = []
-    y_in, s_in, t_in = {}, {}, {}
-    def start_step(i):
-        cut = pl.ds(i * part, part)
-        for r in range(1, groups):
-            to = lax.rem(group + r, groups) * 2 + core
-            source = lax.rem(group + groups - r, groups) * 2 + core
-            for w, (hbm, buf) in enumerate(((kw_hbm, wk), (vw_hbm, wv))):
-                copy = remote(
-                    hbm.at[cut], buf.at[me_dp, cut],
-                    y_send.at[r - 1, i, w], y_recv.at[r - 1, i, w], {"dp": to},
-                )
-                copy.start()
-                started.append(copy)
-                y_in[r, i, w] = remote(
-                    hbm.at[cut], buf.at[source, cut],
-                    y_send.at[r - 1, i, w], y_recv.at[r - 1, i, w], {"dp": to},
-                )
-        for r in range(1, tp):
-            to = lax.rem(me_tp + r, tp)
-            source = lax.rem(me_tp + tp - r, tp)
-            for j in range(pieces):
-                copy = remote(
-                    tok_hbm.at[:, pl.ds(j * deep + i * part, part)],
-                    tok.at[me_tp * pieces + j, :, cut],
-                    t_send.at[r - 1, i, j], t_recv.at[r - 1, i, j], {"tp": to},
-                )
-                copy.start()
-                started.append(copy)
-                t_in[r, i, j] = remote(
-                    tok_hbm.at[:, pl.ds(j * deep + i * part, part)],
-                    tok.at[source * pieces + j, :, cut],
-                    t_send.at[r - 1, i, j], t_recv.at[r - 1, i, j], {"tp": to},
-                )
-
-    start_step(0)
-    for w, (hbm, buf) in enumerate(((kw_hbm, wk), (vw_hbm, wv))):
-        copy = remote(
-            hbm, buf.at[me_dp], s_send.at[w], s_recv.at[w], {"dp": sib}
-        )
+    parity = me_ctx % 2
+    pair = me_ctx + 1 - 2 * parity
+    half = STEPS // 2
+    bufs = ((kw_hbm, wk), (vw_hbm, wv))
+
+    def chunk(k, odd):
+        return pl.ds(pl.multiple_of((2 * k + odd) * part, part), part)
+
+    def begin(copy):
         copy.start()
         started.append(copy)
-        s_in[w] = remote(
-            hbm, buf.at[sib], s_send.at[w], s_recv.at[w], {"dp": sib}
-        )
-    start_step(1)
+
+    def y_copy(r, k, w, owner):
+        hbm, buf = bufs[w]
+        return remote(
+            hbm.at[chunk(k, parity)], buf.at[owner, chunk(k, parity)],
+            y_send.at[r - 1, k, w], y_recv.at[r - 1, k, w],
+            {"dp": lax.rem(group + r, groups) * 2 + core},
+        )
+
+    def z_copy(r, k, w, owner, odd):
+        buf = bufs[w][1]
+        cut = chunk(k, odd)
+        return remote(
+            buf.at[owner, cut], buf.at[owner, cut],
+            z_send.at[r - 1, k, w], z_recv.at[r - 1, k, w], {"ctx": pair},
+        )
+
+    def f_copy(r, k, w, owner, odd, slot):
+        buf = bufs[w][1]
+        cut = chunk(k, odd)
+        return remote(
+            buf.at[owner, cut], buf.at[owner, cut],
+            f_send.at[r - 1, slot, w], f_recv.at[r - 1, slot, w], {"dp": sib},
+        )
+
+    def s_copy(w, owner):
+        hbm, buf = bufs[w]
+        return remote(hbm, buf.at[owner], s_send.at[w], s_recv.at[w], {"dp": sib})
+
+    def t_copy(r, b, j, owner):
+        lines = pl.ds(b * BLOCK, BLOCK)
+        return remote(
+            tok_hbm.at[lines, pl.ds(j * deep, deep)], tok.at[owner * pieces + j, lines, :],
+            t_send.at[r - 1, b, j], t_recv.at[r - 1, b, j], {"tp": lax.rem(me_tp + r, tp)},
+        )
+
+    def source(r, of_core):
+        return lax.rem(group + groups - r, groups) * 2 + of_core
+
+    def start_tokens(b):
+        for r in range(1, tp):
+            for j in range(pieces):
+                begin(t_copy(r, b, j, me_tp))
+
+    for k in range(half):
+        for r in range(1, groups):
+            for w in range(2):
+                begin(y_copy(r, k, w, me_dp))
+        if k == 0:
+            start_tokens(nb - 1)
+            for w in range(2):
+                begin(s_copy(w, me_dp))
 
     def doc_copy(d):
         return remote(
@@ -199,58 +217,62 @@
 
     acc[...] = jnp.zeros_like(acc)
     for w in range(2):
-        s_in[w].wait_recv()
-
-    for i in range(STEPS):
-        cut = pl.ds(i * part, part)
-        forwarded = []
+        s_copy(w, sib).wait_recv()
+
+    for k in range(half):
         for r in range(1, groups):
-            source = lax.rem(group + groups - r, groups) * 2 + core
-            sib_source = lax.rem(group + groups - r, groups) * 2 + (1 - core)
-            for w, buf in enumerate((wk, wv)):
-                y_in[r, i, w].wait_recv()
-                copy = remote(
-                    buf.at[source, cut], buf.at[source, cut],
-                    f_send.at[r - 1, i, w], f_recv.at[r - 1, i, w], {"dp": sib},
-                )
-                copy.start()
-                started.append(copy)
-                forwarded.append(
-                    remote(
-                        buf.at[sib_source, cut], buf.at[sib_source, cut],
-                        f_send.at[r - 1, i, w], f_recv.at[r - 1, i, w], {"dp": sib},
-                    )
-                )
+            for w in range(2):
+                y_copy(r, k, w, source(r, core)).wait_recv()
+                begin(z_copy(r, k, w, source(r, core), parity))
+                begin(f_copy(r, k, w, source(r, core), parity, k))
+    for b in reversed(range(nb)):
         for r in range(1, tp):
+            if b == nb - 1:
+                for j in range(pieces):
+                    t_copy(r, b, j, lax.rem(me_tp + tp - r, tp)).wait_recv()
+        if b == nb - 1:
+            if nb > 1:
+                start_tokens(b - 1)
+            for k in range(half):
+                for r in range(1, groups):
+                    for w in range(2):
+                        z_copy(r, k, w, source(r, core), 1 - parity).wait_recv()
+                        begin(f_copy(r, k, w, source(r, core), 1 - parity, half + k))
+            for k in range(half):
+                for r in range(1, groups):
+                    for w in range(2):
+                        f_copy(r, k, w, source(r, 1 - core), parity, k).wait_recv()
+                        f_copy(r, k, w, source(r, 1 - core), 1 - parity, half + k).wait_recv()
+        lines = slice(b * BLOCK, (b + 1) * BLOCK)
+
+        def add(p):
+            x = tok[p, lines, :]
+            acc[lines, :kvw] += jnp.dot(x, wk[p], preferred_element_type=jnp.float32)
+            acc[lines, kvw:] += jnp.dot(x, wv[p], preferred_element_type=jnp.float32)
+
+        @pl.loop(0, pieces)
+        def _(j):
+            add(me_tp * pieces + j)
+
+        for r in range(1, tp):
+            far = lax.rem(me_tp + tp - r, tp)
             for j in range(pieces):
-                t_in[r, i, j].wait_recv()
-        for copy in forwarded:
-            copy.wait_recv()
-
-        if i + 2 < STEPS:
-            start_step(i + 2)
-
-        @pl.loop(0, dp)
-        def _(p):
-            x = tok[p, :, cut]
-            acc[:, :kvw] += jnp.dot(x, wk[p, cut, :], preferred_element_type=jnp.float32)
-            acc[:, kvw:] += jnp.dot(x, wv[p, cut, :], preferred_element_type=jnp.float32)
-
-    for g in range(kv_heads):
-        u = acc[:, g * HD:(g + 1) * HD]
-        turned = u * cos_ref[...] + pltpu.roll(u, HD // 2, 1) * sin_ref[...]
-        kv[back, g, :, :HD] = turned.astype(jnp.bfloat16)
-        kv[back, g, :, HD:] = acc[:, kvw + g * HD:kvw + (g + 1) * HD].astype(jnp.bfloat16)
-    for d in range(1, back + 1):
+                if b < nb - 1:
+                    t_copy(r, b, j, far).wait_recv()
+                add(far * pieces + j)
+        if 0 < b < nb - 1:
+            start_tokens(b - 1)
+
         for g in range(kv_heads):
-            if d > 1:
-                @pl.when(me_ctx + d - 1 < n_ctx)
+            u = acc[lines, g * HD:(g + 1) * HD]
+            turned = u * cos_ref[lines, :] + pltpu.roll(u, HD // 2, 1) * sin_ref[lines, :]
+            kv[back, g, lines, :HD] = turned.astype(jnp.bfloat16)
+            kv[back, g, lines, HD:] = acc[lines, kvw + g * HD:kvw + (g + 1) * HD].astype(jnp.bfloat16)
+        for d in range(1, back + 1):
+            if d * nb - b < span:
+                @pl.when(me_ctx + d < n_ctx)
                 def _():
-                    kv_copy(kv, kv_send, kv_recv, remote, back, span, nb, rows, g, d - 1, me_ctx + d - 1).wait_send()
-        for g in range(kv_heads):
-            @pl.when(me_ctx + d < n_ctx)
-            def _():
-                kv_copy(kv, kv_send, kv_recv, remote, back, span, nb, rows, g, d, me_ctx + d).start()
+                    kv_copy(kv, kv_send, kv_recv, remote, back, b, d, me_ctx + d).start()
 
     for d in range(1, back + 1):
         @pl.when(me_ctx - d >= 0)
@@ -274,15 +296,15 @@
         keep.append((column <= row) & (key_docs == 0))
 
     group_heads = heads // kv_heads
-    reached = [0] * kv_heads
+    for d in range(1, back + 1):
+        for b in range(nb):
+            if d * nb - b < span:
+                @pl.when(me_ctx - d >= 0)
+                def _():
+                    kv_copy(kv, kv_send, kv_recv, remote, back, b, d, me_ctx - d).wait_recv()
     for b in reversed(range(nb)):
         first = back * nb + b + 1 - span
         for g in range(kv_heads):
-            for d in range(reached[g] + 1, back - first // nb + 1):
-                @pl.when(me_ctx - d >= 0)
-                def _():
-                    kv_copy(kv, kv_send, kv_recv, remote, back, span, nb, rows, g, d, me_ctx - d).wait_recv()
-            reached[g] = max(reached[g], back - first // nb)
             window = jnp.concatenate(
                 [
                     kv[(first + k) // nb, g, ((first + k) % nb) * BLOCK:((first + k) % nb + 1) * BLOCK, :]
@@ -319,17 +341,16 @@
         @pl.when(me_ctx + d < n_ctx)
         def _():
             doc_copy(d).wait_send()
-            if d == back:
-                for g in range(kv_heads):
-                    kv_copy(kv, kv_send, kv_recv, remote, back, span, nb, rows, g, d, me_ctx + d).wait_send()
-
-
-def kv_copy(kv, send, recv, remote, back, span, nb, rows, g, d, other):
-    skip = max(0, d * nb + 1 - span) * BLOCK
-    cut = pl.ds(skip, rows - skip)
+            for b in range(nb):
+                if d * nb - b < span:
+                    kv_copy(kv, kv_send, kv_recv, remote, back, b, d, me_ctx + d).wait_send()
+
+
+def kv_copy(kv, send, recv, remote, back, b, d, other):
+    lines = pl.ds(b * BLOCK, BLOCK)
     return remote(
-        kv.at[back, g, cut], kv.at[back - d, g, cut],
-        send.at[d - 1, g], recv.at[d - 1, g], {"ctx": other},
+        kv.at[back, :, lines], kv.at[back - d, :, lines],
+        send.at[d - 1, b], recv.at[d - 1, b], {"ctx": other},
     )
 
 
@@ -365,11 +386,12 @@
                 pltpu.VMEM((rows, HD), jnp.float32),
                 pltpu.VMEM((rows, HD), jnp.float32),
                 dma((4 + pieces,)),
-                dma((groups - 1, STEPS, 2)), dma((groups - 1, STEPS, 2)),
+                dma((groups - 1, STEPS // 2, 2)), dma((groups - 1, STEPS // 2, 2)),
                 dma((2,)), dma((2,)),
                 dma((groups - 1, STEPS, 2)), dma((groups - 1, STEPS, 2)),
-                dma((tp - 1, STEPS, pieces)), dma((tp - 1, STEPS, pieces)),
-                dma((back, kvw // HD)), dma((back, kvw // HD)),
+                dma((groups - 1, STEPS // 2, 2)), dma((groups - 1, STEPS // 2, 2)),
+                dma((tp - 1, nb, pieces)), dma((tp - 1, nb, pieces)),
+                dma((back, nb)), dma((back, nb)),
                 dma((back,)), dma((back,)),
             ],
             compiler_params=pltpu.CompilerParams(

time: 74.2 us -> 70.3 us (0.947)
  the two profiles are of different devices: /device:TPU:0 before, /device:TPU:8 now
where the time goes in v3:
time: 70.3 us; the launch traced here: 70.2 us
  Pallas kernels  67 us (95%)
  local copies, waits for them, and re-layouts  3.13 us (4%)
    pallas_call x1, Pallas kernels, body(): pl.pallas_call(functools.partial(kernel, (dp, n_ctx, tp)), out_shape=jax....  67 us
    unnamed x1, local copies, waits for them, and re-layouts  3.13 us

profile of v3, /device:TPU:8, one launch (start us, length us, event | category | flops | bytes accessed | tf_op | source)
XLA Modules:
  0.0 70.2 jit_solution(6456090358257112218)
XLA Ops:
  0.0 67.0 %shard_map.55 = bf16[256,4096]{1,0:T(8,128)(2,1)} custom-call(bf16[256,4096]{1,0:T(8,128)(2,1)} %bitcast.4, bf16[256,4096]{1,0:T(8,128)(2,1)} %bitcast.5, bf16[2048,256]{1,0:T(8,128)(2,1)} %kw_hbm.1, bf16[2048,256]{1,0:T(8,128)(2,1)} %vw_hbm.1, s32[1,2]{1,0:T(1,128)} %docs_hbm.1), custom_call_target="tpu_custom_call" | custom-call | tf_op jit(solution)/shard_map/pallas_call | solution.py:371
  67.1 3.1 %copy.7 = bf16[1,256,4096]{2,1,0:T(8,128)(2,1)} copy(bf16[1,256,4096]{2,1,0:T(8,128)(2,1)} %bitcast.3) | data formatting | bytes 4194304
